TPU v7x, 32 devices: a whole 2x2x4 slice. The times are simulated.
32 devices in a mesh: band: 2 (over x), stn: 8 (over z, y), tm: 2 (over core).
Axes of the slice: x: 2, y: 2, z: 4, core: 2. Of those that a mesh axis runs over, the one named last changes fastest.
Arguments:
- voltages: int32 [704, 4, 32768], P('stn', 'band', 'tm'), parts along dimension 1, may hold values from -125 to 125, as said below
- filter_taps: float32 [16, 128], replicated, may hold values from -0.036 to 0.036
Outputs:
- visibilities: float32 [2, 2, 128, 704, 704], P(None, None, ('band', 'stn', 'tm')), parts along dimension 2
There are 2 independent parts, one for each index of `band`. A program takes and returns all parts, laid end to end along the dimension named above; an argument that names none is the same for every part. Nothing has to cross between parts.
Inputs may be any that keep to these rules, and one draw needn't show every extreme that they name: `voltages`: each input's samples are an integer gain of -2 to 2 times a signal common to all inputs plus noise of its own.
All inputs are finite; a program needn't handle non-finite values.
Results may differ from a plain program's by a relative error of at most 0.00049.
Values may be sent and summed in bfloat16 or wider, within the bound.
A program may use at most 192 MiB of HBM per device.

v0:
```python
import math
import jax
import jax.numpy as jnp
from jax import lax
from jax.sharding import PartitionSpec as P


def passed_along(value, axis, steps):
    count = lax.axis_size(axis)
    pairs = [(source, (source + steps) % count) for source in range(count)]
    return lax.ppermute(value, axis, pairs)


def transform_table(frame_len, chan_count):
    sample_index = jnp.arange(frame_len, dtype=jnp.int32)[:, None]
    chan_index = jnp.arange(chan_count, dtype=jnp.int32)[None, :]
    phase = (2 * chan_index + 1) * sample_index % (2 * frame_len)
    angle = phase.astype(jnp.float32) * (math.pi / frame_len)
    factor = 1.0 / math.sqrt(frame_len)
    cosine = jnp.cos(angle) * factor
    sine = -jnp.sin(angle) * factor
    return jnp.stack([cosine, sine], axis=2).reshape(frame_len, 2 * chan_count)


def arrange(blocks):
    stations, blocks_time, per_dev, parts_two, inputs_dev, sub_count, spec_dev = blocks.shape
    ordered = jnp.transpose(blocks, (3, 5, 2, 0, 4, 1, 6))
    return ordered.reshape(
        parts_two, sub_count, per_dev, stations * inputs_dev, blocks_time * spec_dev
    )


def correlate(stacked):
    real_in = stacked[0]
    imag_in = stacked[1]
    right_side = jnp.concatenate([real_in, imag_in], axis=-1)
    left_imag = jnp.concatenate([imag_in, -real_in], axis=-1)
    real_part = jnp.einsum(
        "gcis,gcjs->gcij", right_side, right_side, preferred_element_type=jnp.float32
    )
    imag_part = jnp.einsum(
        "gcis,gcjs->gcij", left_imag, right_side, preferred_element_type=jnp.float32
    )
    return jnp.stack([real_part, imag_part])


def shards(voltages, filter_taps):
    inputs_dev, sub_count, time_dev = voltages.shape
    taps_count, frame_len = filter_taps.shape
    spec_dev = time_dev // frame_len
    chan_count = frame_len // 2
    lagging = taps_count - 1
    frames = voltages.astype(jnp.bfloat16).reshape(inputs_dev, sub_count, spec_dev, frame_len)
    last_frames = frames[:, :, spec_dev - lagging :, :]
    received = passed_along(last_frames, "tm", 1)
    earlier = jnp.concatenate([jnp.zeros_like(received[:, :1]), received[:, :-1]], axis=1)
    history = jnp.where(lax.axis_index("tm") == 0, earlier, received)
    extended = jnp.concatenate([history, frames], axis=2).astype(jnp.float32)
    filtered = filter_taps[0] * extended[:, :, 0:spec_dev]
    for tap_index in range(1, taps_count):
        filtered = (
            filtered + filter_taps[tap_index] * extended[:, :, tap_index : tap_index + spec_dev]
        )
    table = transform_table(frame_len, chan_count)
    spectra = lax.dot_general(
        table,
        filtered.reshape(-1, frame_len),
        (((0,), (1,)), ((), ())),
        precision=lax.Precision.HIGHEST,
        preferred_element_type=jnp.float32,
    ).astype(jnp.bfloat16)
    stations = lax.axis_size("stn")
    halves = lax.axis_size("tm")
    scale = 1.0 / (spec_dev * halves)
    moved = lax.all_to_all(spectra[None], ("stn", "tm"), split_axis=1, concat_axis=0, tiled=True)
    per_dev = moved.shape[1] // 2
    blocks = moved.reshape(stations, halves, per_dev, 2, inputs_dev, sub_count, spec_dev)
    result = correlate(arrange(blocks))
    return result * scale


def solution(mesh):
    placed = (P("stn", "band", "tm"), P())
    return jax.shard_map(
        shards,
        mesh=mesh,
        in_specs=placed,
        out_specs=P(None, None, ("band", "stn", "tm"), None, None),
        check_vma=False,
    )
```

profile of v0, /device:TPU:1, one launch (start us, length us, event | category | flops | bytes accessed | tf_op | source)
XLA Modules:
  0.0 507.7 jit_solution(10586503539075918280)
XLA Ops:
  0.0 9.0 %convert_element_type.26 = bf16[88,2,16384]{2,1,0:T(2,128)(2,1)} convert(s32[88,2,16384]{2,1,0:T(2,128)} %param.2) | non-fusion elementwise | flops 2883584 | bytes 17301504 | tf_op jit(solution)/shard_map/convert_element_type | solution.py:53
  9.0 0.0 copy-start.1
  9.0 10.5 %reshape.154 = bf16[88,2,128,128]{3,2,1,0:T(8,128)(2,1)} reshape(bf16[88,2,16384]{2,1,0:T(2,128)(2,1)} %convert_element_type.26) | data formatting | bytes 11534336 | tf_op jit(solution)/shard_map/reshape | solution.py:53
  19.5 1.4 slice.146
  20.9 0.1 copy.33
  21.1 0.2 copy.19
  21.3 0.1 collective-permute-start
  21.4 0.2 cosine_multiply_fusion
  21.6 0.1 copy.17
  21.7 0.0 copy-done.1
  21.7 1.7 collective-permute-done
  23.5 0.1 copy.28
  23.6 0.2 pad_select_fusion
  23.7 10.6 %maximum_convert_fusion = f32[88,2,143,128]{3,2,0,1:T(8,128)} fusion(bf16[88,2,15,128]{3,2,0,1:T(8,128)(2,1)S(1)} %pad_select_fusion, bf16[88,2,128,128]{3,2,1,0:T(8,128)(2,1)} %reshape.154), kind=kLoop, calls=%fused_computation.36 | loop fusion | flops 12886016 | bytes 19329024 | tf_op jit(solution)/shard_map/convert_element_type | solution.py:58
  34.3 74.6 %fusion.1 = f32[88,2,128,128]{3,2,0,1:T(8,128)} fusion(f32[88,2,143,128]{3,2,0,1:T(8,128)} %maximum_convert_fusion, f32[128]{0:T(128)S(1)} %get-tuple-element.23, f32[128]{0:T(128)S(1)} %get-tuple-element.24, f32[128]{0:T(128)S(1)} %get-tuple-element.10, f32[128]{0:T(128)S(1)} %get-tuple-element.11, f32[128]{0:T(128)S(1)} %get-tuple-element.12, ...), kind=kLoop, calls=%fused_computation.4 | loop fusion | flops 89391104 | bytes 196091904 | tf_op jit(solution)/shard_map/add | solution.py:62
  109.0 10.6 %copy.22 = f32[88,2,128,128]{3,2,1,0:T(8,128)} copy(f32[88,2,128,128]{3,2,0,1:T(8,128)} %fusion.1) | data formatting | bytes 23068672 | tf_op jit(solution)/shard_map/add | solution.py:62
  119.6 13.6 %fusion = bf16[1,128,22528]{2,1,0:T(8,128)(2,1)S(1)} fusion(f32[128,128]{0,1:T(8,128)S(1)} %bitcast.54, f32[22528,128]{1,0:T(8,128)} %bitcast.52), kind=kOutput, calls=%fused_computation.2 | convolution fusion | flops 4432068608 | bytes 17367040 | tf_op jit(solution)/shard_map/dot_general | solution.py:65
  133.2 47.5 %copy.32 = bf16[1,128,22528]{2,0,1:T(2,128)(2,1)} copy(bf16[1,128,22528]{2,1,0:T(8,128)(2,1)S(1)} %fusion) | data formatting | bytes 11534336 | tf_op jit(solution)/shard_map/broadcast_in_dim | solution.py:75
  180.7 0.6 broadcast.142
  181.3 35.9 %reduce.2 = bf16[128,22528]{1,0:T(8,128)(2,1)} reduce(bf16[128,1,22528]{2,1,0:T(2,128)(2,1)} %bitcast.51, bf16[]{:T(256)} %broadcast.142), dimensions={1}, to_apply=%bitcast.50.reduce_sub_computation | reduce | bytes 11534338
  217.2 13.4 %reshape.156 = bf16[16,2,90112]{2,1,0:T(2,128)(2,1)} reshape(bf16[128,22528]{1,0:T(8,128)(2,1)} %reduce.2) | data formatting | bytes 11534336
  230.5 133.9 %all_to_all.4 = bf16[16,2,90112]{2,1,0:T(2,128)(2,1)} all-to-all(bf16[16,2,90112]{2,1,0:T(2,128)(2,1)} %reshape.156), channel_id=1, replica_groups=mesh['band'=2,'stn'=8,'tm'=2] {'stn','tm'}, dimensions={0} | all-to-all | bytes 11534336 | tf_op jit(solution)/shard_map/all_to_all | solution.py:75
  364.5 13.8 %reshape.157 = bf16[128,1,22528]{2,1,0:T(2,128)(2,1)} reshape(bf16[16,2,90112]{2,1,0:T(2,128)(2,1)} %all_to_all.4) | data formatting | bytes 11534336
  378.3 36.0 %bitcast_reduce_fusion = bf16[128,22528]{1,0:T(8,128)(2,1)} fusion(bf16[128,1,22528]{2,1,0:T(2,128)(2,1)} %reshape.157), kind=kLoop, calls=%fused_computation.75 | loop fusion | bytes 11534336 | tf_op jit(solution)/shard_map/all_to_all | solution.py:75
  414.3 8.9 %reshape.153 = bf16[8,2,4,2,88,2,128]{6,5,4,3,2,1,0:T(2,128)(2,1)} reshape(bf16[128,22528]{1,0:T(8,128)(2,1)} %bitcast_reduce_fusion) | data formatting | bytes 11534336 | tf_op jit(solution)/shard_map/reshape | solution.py:77
  423.2 8.4 %fusion.26 = (bf16[1,2,4,8,88,2,128]{6,1,4,0,2,5,3:T(2,128)(2,1)S(1)}, bf16[1,2,4,8,88,2,128]{6,1,4,0,2,5,3:T(2,128)(2,1)}) fusion(bf16[2,2,4,8,88,2,128]{6,1,4,0,2,5,3:T(2,128)(2,1)} %bitcast.53), kind=kLoop, calls=%fused_computation.73 | loop fusion | bytes 11534336 | tf_op jit(solution)/shard_map/slice | solution.py:35
  431.7 4.5 copy.25
  436.2 6.5 %squeeze.7 = bf16[2,4,704,256]{3,2,1,0:T(8,128)(2,1)S(1)} reshape(bf16[1,2,4,8,88,2,128]{6,5,4,3,2,1,0:T(2,128)(2,1)} %copy.25) | data formatting | bytes 5767168 | tf_op jit(solution)/shard_map/squeeze | solution.py:35
  442.8 6.4 %copy.24 = bf16[1,2,4,8,88,2,128]{6,5,4,3,2,1,0:T(2,128)(2,1)} copy(bf16[1,2,4,8,88,2,128]{6,1,4,0,2,5,3:T(2,128)(2,1)} %get-tuple-element.6) | data formatting | bytes 5767168 | tf_op jit(solution)/shard_map/slice | solution.py:34
  449.1 7.4 %squeeze.6 = bf16[2,4,704,256]{3,2,1,0:T(8,128)(2,1)} reshape(bf16[1,2,4,8,88,2,128]{6,5,4,3,2,1,0:T(2,128)(2,1)} %copy.24) | data formatting | bytes 5767168 | tf_op jit(solution)/shard_map/squeeze | solution.py:34
  456.6 5.0 fusion.27
  461.6 0.2 constant_dynamic-update-slice_fusion
  461.8 0.0 copy-start
  461.9 8.4 %convolution_bitcast_fusion.1 = f32[1,2,4,704,704]{4,3,2,1,0:T(8,128)} fusion(bf16[2,4,704,512]{3,2,1,0:T(8,128)(2,1)S(1)} %constant_dynamic-update-slice_fusion), kind=kOutput, calls=%fused_computation.35 | convolution fusion | flops 4060086272 | bytes 21626880 | tf_op jit(solution)/shard_map/gcis,gcjs->gcij/dot_general | solution.py:38
  470.3 0.0 copy-done
  470.3 14.1 %convolution_bitcast_fusion = f32[1,2,4,704,704]{4,3,2,1,0:T(8,128)} fusion(bf16[2,4,704,512]{3,2,1,0:T(8,128)(2,1)} %copy-done, bf16[2,4,704,256]{3,2,1,0:T(8,128)(2,1)} %get-tuple-element.7, bf16[2,4,704,256]{3,2,1,0:T(8,128)(2,1)S(1)} %squeeze.7), kind=kOutput, calls=%fused_computation.34 | convolution fusion | flops 4071620608 | bytes 27394048 | tf_op jit(solution)/shard_map/gcis,gcjs->gcij/dot_general | solution.py:41
  484.4 23.2 %maximum_multiply_fusion = f32[2,2,4,704,704]{4,3,2,1,0:T(8,128)} fusion(f32[1,2,4,704,704]{4,3,2,1,0:T(8,128)} %convolution_bitcast_fusion, f32[1,2,4,704,704]{4,3,2,1,0:T(8,128)} %convolution_bitcast_fusion.1), kind=kLoop, calls=%fused_computation | loop fusion | flops 15859712 | bytes 63438848 | tf_op jit(solution)/shard_map/mul | solution.py:79
  (4 shorter events, 0.0 us)
Async XLA Ops:
  9.0 12.7 %copy-start.1 = (f32[16,128]{1,0:T(8,128)S(1)}, f32[16,128]{1,0:T(8,128)}, u32[]{:S(2)}) copy-start(f32[16,128]{1,0:T(8,128)} %param.3) | copy-start | bytes 24580
  21.3 2.2 collective-permute-start
  461.8 8.4 %copy-start = (bf16[2,4,704,512]{3,2,1,0:T(8,128)(2,1)}, bf16[2,4,704,512]{3,2,1,0:T(8,128)(2,1)S(1)}, u32[]{:S(2)}) copy-start(bf16[2,4,704,512]{3,2,1,0:T(8,128)(2,1)S(1)} %constant_dynamic-update-slice_fusion) | copy-start | bytes 17301508
where the time goes:
time: 516 us; the launch traced here: 508 us
  local copies, waits for them, and re-layouts  177 us (34%)
  other arithmetic  159 us (31%)
  blocking collectives  134 us (26%)
  matrix products  36.1 us (7%)
    all_to_all x1, blocking collectives, shards(): lax.all_to_all(spectra[None], ('stn', 'tm'), split_axis=1, concat_axis=0,...  134 us
    add x1, other arithmetic, shards(): filtered + filter_taps[tap_index] * extended[:, :, tap_index:tap_index +...  74.6 us
    broadcast_in_dim x1, local copies, waits for them, and re-layouts, shards(): spectra[None]  47.5 us
    all_to_all x1, local copies, waits for them, and re-layouts, shards(): lax.all_to_all(spectra[None], ('stn', 'tm'), split_axis=1, concat_axis=0,...  36 us
    unnamed x1, other arithmetic  35.9 us
    unnamed x9, local copies, waits for them, and re-layouts  28 us
    mul x1, other arithmetic, shards(): return result * scale  23.2 us
    dot_general x1, matrix products, correlate(): jnp.einsum('gcis,gcjs->gcij', left_imag, right_side, preferred_element_ty...  14.1 us
  transfers between devices with their start and end apart: 1, of which 1 were waited for; matrix products, arithmetic and copies ran while one was open for 0% of the time, Pallas kernels for 0%

commit v1 on v0

--- a/solution.py
+++ b/solution.py
@@ -72,7 +72,15 @@
     stations = lax.axis_size("stn")
     halves = lax.axis_size("tm")
     scale = 1.0 / (spec_dev * halves)
-    moved = lax.all_to_all(spectra[None], ("stn", "tm"), split_axis=1, concat_axis=0, tiled=True)
+    moved = jnp.concatenate(
+        lax.all_to_all(
+            jnp.stack(jnp.split(spectra[None], lax.axis_size(("stn", "tm")), axis=1)),
+            ("stn", "tm"),
+            0,
+            0,
+        ),
+        axis=0,
+    )
     per_dev = moved.shape[1] // 2
     blocks = moved.reshape(stations, halves, per_dev, 2, inputs_dev, sub_count, spec_dev)
     result = correlate(arrange(blocks))

time: 516 us -> 361 us (0.70); the launches traced: 508 us -> 360 us
  local copies, waits for them, and re-layouts: 177 us -> 66 us
  other arithmetic: 159 us -> 123 us
    broadcast_in_dim x1 -> x0, local copies, waits for them, and re-layouts: 47.5 us -> none  [shards(): spectra[None]]
    all_to_all x1 -> x0, local copies, waits for them, and re-layouts: 36 us -> none  [shards(): lax.all_to_all(spectra[None], ('stn', 'tm'), split_axis=1, concat_axis=0,...]
    unnamed x1 -> x0, other arithmetic: 35.9 us -> none
    unnamed x9 -> x21, local copies, waits for them, and re-layouts: 28 us -> 0.58 us
    another operation x0 -> x2, local copies, waits for them, and re-layouts: none -> 8.92 us  [the longest x1 8.89 us: shards(): moved.reshape(stations, halves, per_dev, 2, inputs_dev, sub_count, spec_dev)]
    reshape x1 -> x0, local copies, waits for them, and re-layouts: 8.89 us -> none  [shards(): moved.reshape(stations, halves, per_dev, 2, inputs_dev, sub_count, spec_dev)]
where the time goes in v1:
time: 361 us; the launch traced here: 360 us
  blocking collectives  134 us (37%)
  other arithmetic  123 us (34%)
  local copies, waits for them, and re-layouts  66 us (18%)
  matrix products  35.6 us (10%)
    all_to_all x1, blocking collectives, shards(): lax.all_to_all(jnp.stack(jnp.split(spectra[None], lax.axis_size(('stn', '...  134 us
    add x1, other arithmetic, shards(): filtered + filter_taps[tap_index] * extended[:, :, tap_index:tap_index +...  74.6 us
    mul x1, other arithmetic, shards(): return result * scale  23.2 us
    dot_general x1, matrix products, correlate(): jnp.einsum('gcis,gcjs->gcij', left_imag, right_side, preferred_element_ty...  14.1 us
    dot_general x1, matrix products, shards(): lax.dot_general(table, filtered.reshape(-1, frame_len), (((0,), (1,)), ((...  13.1 us
    slice x2, local copies, waits for them, and re-layouts, correlate(): imag_in = stacked[1]  13 us
    add x1, local copies, waits for them, and re-layouts, shards(): filtered + filter_taps[tap_index] * extended[:, :, tap_index:tap_index +...  10.6 us
    convert_element_type x1, other arithmetic, shards(): extended = jnp.concatenate([history, frames], axis=2).astype(jnp.float32)  10.6 us
  transfers between devices with their start and end apart: 1, of which 1 were waited for; matrix products, arithmetic and copies ran while one was open for 0% of the time, Pallas kernels for 0%

profile of v1, /device:TPU:1, one launch (start us, length us, event | category | flops | bytes accessed | tf_op | source)
XLA Modules:
  0.0 360.1 jit_solution(6691284587719321015)
XLA Ops:
  0.0 9.0 %convert_element_type.26 = bf16[88,2,16384]{2,1,0:T(2,128)(2,1)} convert(s32[88,2,16384]{2,1,0:T(2,128)} %param.2) | non-fusion elementwise | flops 2883584 | bytes 17301504 | tf_op jit(solution)/shard_map/convert_element_type | solution.py:53
  9.0 0.0 copy-start.1
  9.0 10.5 %reshape.146 = bf16[88,2,128,128]{3,2,1,0:T(8,128)(2,1)} reshape(bf16[88,2,16384]{2,1,0:T(2,128)(2,1)} %convert_element_type.26) | data formatting | bytes 11534336 | tf_op jit(solution)/shard_map/reshape | solution.py:53
  19.5 1.4 slice.146
  20.9 0.1 copy.29
  21.1 0.2 copy.18
  21.3 0.1 collective-permute-start
  21.4 0.2 cosine_multiply_fusion
  21.6 0.1 copy.16
  21.7 0.0 copy-done.1
  21.7 1.7 collective-permute-done
  23.5 0.1 copy.26
  23.5 0.2 pad_select_fusion
  23.7 10.6 %maximum_convert_fusion = f32[88,2,143,128]{3,2,0,1:T(8,128)} fusion(bf16[88,2,15,128]{3,2,0,1:T(8,128)(2,1)S(1)} %pad_select_fusion, bf16[88,2,128,128]{3,2,1,0:T(8,128)(2,1)} %reshape.146), kind=kLoop, calls=%fused_computation.36 | loop fusion | flops 12886016 | bytes 19329024 | tf_op jit(solution)/shard_map/convert_element_type | solution.py:58
  34.3 74.6 %fusion.1 = f32[88,2,128,128]{3,2,0,1:T(8,128)} fusion(f32[88,2,143,128]{3,2,0,1:T(8,128)} %maximum_convert_fusion, f32[128]{0:T(128)S(1)} %get-tuple-element.23, f32[128]{0:T(128)S(1)} %get-tuple-element.24, f32[128]{0:T(128)S(1)} %get-tuple-element.10, f32[128]{0:T(128)S(1)} %get-tuple-element.11, f32[128]{0:T(128)S(1)} %get-tuple-element.12, ...), kind=kLoop, calls=%fused_computation.4 | loop fusion | flops 89391104 | bytes 196091904 | tf_op jit(solution)/shard_map/add | solution.py:62
  108.9 10.6 %copy.21 = f32[88,2,128,128]{3,2,1,0:T(8,128)} copy(f32[88,2,128,128]{3,2,0,1:T(8,128)} %fusion.1) | data formatting | bytes 23068672 | tf_op jit(solution)/shard_map/add | solution.py:62
  119.6 13.1 %fusion = bf16[1,128,22528]{2,1,0:T(8,128)(2,1)S(1)} fusion(f32[128,128]{0,1:T(8,128)S(1)} %bitcast.114, f32[22528,128]{1,0:T(8,128)} %bitcast.112), kind=kOutput, calls=%fused_computation.2 | convolution fusion | flops 4432068608 | bytes 17367040 | tf_op jit(solution)/shard_map/dot_general | solution.py:65
  133.2 133.6 %all_to_all.5 = bf16[16,1,8,22528]{3,2,1,0:T(8,128)(2,1)} all-to-all(bf16[16,1,8,22528]{3,2,1,0:T(8,128)(2,1)S(1)} %fusion.19), channel_id=1, replica_groups=mesh['band'=2,'stn'=8,'tm'=2] {'stn','tm'}, dimensions={0} | all-to-all | bytes 11534336 | tf_op jit(solution)/shard_map/all_to_all | solution.py:76
  266.8 8.9 %reshape_reshape.3 = bf16[8,2,4,2,88,2,128]{6,5,4,3,2,1,0:T(2,128)(2,1)} reshape(bf16[16,1,8,22528]{3,2,1,0:T(8,128)(2,1)} %all_to_all.5) | data formatting | bytes 11534336 | tf_op jit(solution)/shard_map/reshape;reshape | solution.py:85
  275.7 8.5 %fusion.42 = (bf16[1,2,4,8,88,2,128]{6,1,4,0,2,5,3:T(2,128)(2,1)S(1)}, bf16[1,2,4,8,88,2,128]{6,1,4,0,2,5,3:T(2,128)(2,1)}) fusion(bf16[2,2,4,8,88,2,128]{6,1,4,0,2,5,3:T(2,128)(2,1)} %bitcast.113), kind=kLoop, calls=%fused_computation.105 | loop fusion | bytes 11534336 | tf_op jit(solution)/shard_map/slice | solution.py:35
  284.2 4.5 %copy.23 = bf16[1,2,4,8,88,2,128]{6,5,4,3,2,1,0:T(2,128)(2,1)} copy(bf16[1,2,4,8,88,2,128]{6,1,4,0,2,5,3:T(2,128)(2,1)S(1)} %get-tuple-element.5) | data formatting | bytes 5767168 | tf_op jit(solution)/shard_map/slice | solution.py:35
  288.7 6.6 %squeeze.7 = bf16[2,4,704,256]{3,2,1,0:T(8,128)(2,1)S(1)} reshape(bf16[1,2,4,8,88,2,128]{6,5,4,3,2,1,0:T(2,128)(2,1)} %copy.23) | data formatting | bytes 5767168 | tf_op jit(solution)/shard_map/squeeze | solution.py:35
  295.3 6.4 %copy.22 = bf16[1,2,4,8,88,2,128]{6,5,4,3,2,1,0:T(2,128)(2,1)} copy(bf16[1,2,4,8,88,2,128]{6,1,4,0,2,5,3:T(2,128)(2,1)} %get-tuple-element.6) | data formatting | bytes 5767168 | tf_op jit(solution)/shard_map/slice | solution.py:34
  301.7 7.4 %squeeze.6 = bf16[2,4,704,256]{3,2,1,0:T(8,128)(2,1)} reshape(bf16[1,2,4,8,88,2,128]{6,5,4,3,2,1,0:T(2,128)(2,1)} %copy.22) | data formatting | bytes 5767168 | tf_op jit(solution)/shard_map/squeeze | solution.py:34
  309.1 5.0 %fusion.43 = (bf16[2,4,704,256]{3,2,1,0:T(8,128)(2,1)}, bf16[2,4,704,512]{3,2,1,0:T(8,128)(2,1)S(1)}) fusion(bf16[2,4,704,256]{3,2,1,0:T(8,128)(2,1)} %squeeze.6), kind=kLoop, calls=%fused_computation.106 | loop fusion | flops 4325375 | bytes 8650752 | tf_op jit(solution)/shard_map/neg | solution.py:37
  314.2 0.2 constant_dynamic-update-slice_fusion
  314.4 0.0 copy-start
  314.4 8.4 %convolution_bitcast_fusion.1 = f32[1,2,4,704,704]{4,3,2,1,0:T(8,128)} fusion(bf16[2,4,704,512]{3,2,1,0:T(8,128)(2,1)S(1)} %constant_dynamic-update-slice_fusion), kind=kOutput, calls=%fused_computation.35 | convolution fusion | flops 4060086272 | bytes 21626880 | tf_op jit(solution)/shard_map/gcis,gcjs->gcij/dot_general | solution.py:38
  322.8 0.0 copy-done
  322.8 14.1 %convolution_bitcast_fusion = f32[1,2,4,704,704]{4,3,2,1,0:T(8,128)} fusion(bf16[2,4,704,512]{3,2,1,0:T(8,128)(2,1)} %copy-done, bf16[2,4,704,256]{3,2,1,0:T(8,128)(2,1)} %get-tuple-element.7, bf16[2,4,704,256]{3,2,1,0:T(8,128)(2,1)S(1)} %squeeze.7), kind=kOutput, calls=%fused_computation.34 | convolution fusion | flops 4071620608 | bytes 27394048 | tf_op jit(solution)/shard_map/gcis,gcjs->gcij/dot_general | solution.py:41
  336.9 23.2 %maximum_multiply_fusion = f32[2,2,4,704,704]{4,3,2,1,0:T(8,128)} fusion(f32[1,2,4,704,704]{4,3,2,1,0:T(8,128)} %convolution_bitcast_fusion, f32[1,2,4,704,704]{4,3,2,1,0:T(8,128)} %convolution_bitcast_fusion.1), kind=kLoop, calls=%fused_computation | loop fusion | flops 15859712 | bytes 63438848 | tf_op jit(solution)/shard_map/mul | solution.py:87
  (20 shorter events, 0.5 us)
Async XLA Ops:
  9.0 12.7 %copy-start.1 = (f32[16,128]{1,0:T(8,128)S(1)}, f32[16,128]{1,0:T(8,128)}, u32[]{:S(2)}) copy-start(f32[16,128]{1,0:T(8,128)} %param.3) | copy-start | bytes 24580
  21.3 2.2 collective-permute-start
  314.4 8.4 %copy-start = (bf16[2,4,704,512]{3,2,1,0:T(8,128)(2,1)}, bf16[2,4,704,512]{3,2,1,0:T(8,128)(2,1)S(1)}, u32[]{:S(2)}) copy-start(bf16[2,4,704,512]{3,2,1,0:T(8,128)(2,1)S(1)} %constant_dynamic-update-slice_fusion) | copy-start | bytes 17301508
